TPU v7x, 512 devices: a whole 4x8x8 slice. The times are simulated.
512 devices in a mesh: az: 16 (over x, z_lo, core), lat: 8 (over y), ta: 4 (over z_hi).
Axes of the slice: x: 4, y: 8, z: 8 (z_hi: 4, z_lo: 2; z = z_hi * 2 + z_lo), core: 2. Of those that a mesh axis runs over, the one named last changes fastest.
Arguments:
- queries: bfloat16 [4, 128, 256, 1024], P('ta', 'lat', 'az'), may hold values from -8 to 8
- keys_values: bfloat16 [2, 4, 128, 256, 1024], P(None, 'ta', 'lat', 'az'), may hold values from -8 to 8
- windows: int32 [4, 16, 32, 15], P('ta', 'lat', 'az'), may hold values from -1 to 2047, as said below
Outputs:
- attended: bfloat16 [4, 128, 256, 1024], P('ta', 'lat', 'az')
Inputs may be any that keep to these rules, and one draw needn't show every extreme that they name: Each row windows[f, r, c] lists distinct tiles, the tile (f, r, c) among them; every other listed tile is in frame f and at most two tile columns away around the azimuth loop in tile row r, or at most two tile rows away in tile column c, or at most one tile row and one tile column away, or it is tile (f - 1, r, c) or (f + 1, r, c). Tile rows never wrap across the poles. -1 marks an empty slot.
All inputs are finite; a program needn't handle non-finite values.
Results may differ from a plain program's by a relative error of at most 0.0027.
Values may be sent and summed in bfloat16 or wider, within the bound.
A program may use at most 64 MiB of HBM per device.

v0:
```python
import math

import jax
import jax.numpy as jnp
from jax import lax
from jax.sharding import PartitionSpec as P

HD = 128
TS = 8


def extended(cells, sides, width, closed):
    for axis, dim in sides:
        count = lax.axis_size(axis)
        ends = count if closed else count - 1
        head = lax.slice_in_dim(cells, 0, width, axis=dim)
        tail = lax.slice_in_dim(cells, cells.shape[dim] - width, cells.shape[dim], axis=dim)
        cells = jnp.concatenate(
            [
                lax.ppermute(tail, axis, [(i, (i + 1) % count) for i in range(ends)]),
                cells,
                lax.ppermute(head, axis, [((i + 1) % count, i) for i in range(ends)]),
            ],
            axis=dim,
        )
    return cells


def tile_split(field, row_count, col_count):
    outer_shape = field.shape[:-3]
    channels = field.shape[-1]
    extra_dims = len(outer_shape)
    shaped = field.reshape(outer_shape + (row_count, TS, col_count, TS, channels))
    axis_order = tuple(range(extra_dims)) + (
        extra_dims,
        extra_dims + 2,
        extra_dims + 1,
        extra_dims + 3,
        extra_dims + 4,
    )
    return shaped.transpose(axis_order).reshape(
        outer_shape + (row_count * col_count, TS * TS, channels)
    )


def soft_weights(scores, allowed):
    masked = jnp.where(allowed, scores, -jnp.inf)
    peak_score = jnp.max(masked, axis=-1, keepdims=True)
    weights = jnp.exp(masked - peak_score)
    weight_sum = jnp.sum(weights, axis=-1, keepdims=True)
    return (weights.astype(jnp.bfloat16), weight_sum)


def attend_block(
    query_block,
    plane_block,
    frames_block,
    window_block,
    row_first,
    col_first,
    frame_here,
    rows_all,
    cols_all,
):
    rows_here, cols_here, slot_count = window_block.shape
    head_count = query_block.shape[-1] // HD
    tokens = TS * TS
    span_rows = rows_here + 4
    span_cols = cols_here + 4
    plane_tiles = span_rows * span_cols
    own_tiles = rows_here * cols_here
    tile_ids = window_block.reshape(own_tiles, slot_count)
    filled = tile_ids >= 0
    clamped = jnp.maximum(tile_ids, 0)
    frame_of = clamped // (rows_all * cols_all)
    row_of = clamped // cols_all % rows_all
    col_of = clamped % cols_all
    row_step = row_of - row_first
    in_plane = (row_step + 2) * span_cols + (col_of - col_first + 2) % cols_all
    in_block = row_step * cols_here + (col_of - col_first) % cols_all
    frame_step = frame_of - frame_here
    position = jnp.where(
        frame_step == 0,
        in_plane,
        jnp.where(frame_step < 0, plane_tiles + in_block, plane_tiles + own_tiles + in_block),
    )
    position = jnp.where(filled, position, 0)
    query_tiles = tile_split(query_block, rows_here, cols_here)
    plane_all = tile_split(plane_block, span_rows, span_cols)
    frame_all = tile_split(frames_block, rows_here, cols_here).reshape(
        2, 2 * own_tiles, tokens, plane_block.shape[-1]
    )
    pool_all = jnp.concatenate([plane_all, frame_all], axis=1)
    score_scale = 1.0 / math.sqrt(HD)
    pieces = []
    for head_index in range(head_count):
        columns = slice(head_index * HD, (head_index + 1) * HD)
        key_pool = pool_all[..., columns]
        query_part = query_tiles[:, :, columns]
        key_block = key_pool[0][position].reshape(own_tiles, slot_count * tokens, HD)
        value_block = key_pool[1][position].reshape(own_tiles, slot_count * tokens, HD)
        scores = (
            jnp.einsum("tqd,tkd->tqk", query_part, key_block, preferred_element_type=jnp.float32)
            * score_scale
        )
        allowed = jnp.repeat(filled, tokens, axis=1)[:, None, :]
        rounded, weight_sum = soft_weights(scores, allowed)
        summed = jnp.einsum(
            "tqk,tkd->tqd", rounded, value_block, preferred_element_type=jnp.float32
        )
        pieces.append((summed / weight_sum).astype(jnp.bfloat16))
    joined = jnp.concatenate(pieces, axis=-1)
    shaped = joined.reshape(rows_here, cols_here, TS, TS, head_count * HD)
    return shaped.transpose(0, 2, 1, 3, 4).reshape(rows_here * TS, cols_here * TS, head_count * HD)


def local(queries, keys_values, windows):
    rows_here = windows.shape[1]
    cols_here = windows.shape[2]
    lat_count = lax.axis_size("lat")
    rows_all = rows_here * lat_count
    cols_all = cols_here * lax.axis_size("az")
    frame_here = lax.axis_index("ta")
    col_first = lax.axis_index("az") * cols_here
    plane_kv = extended(keys_values, (("az", 3), ("lat", 2)), 2 * TS, True)
    frames_near = extended(keys_values, (("ta", 1),), 1, False)
    row_first = lax.axis_index("lat") * rows_here
    result = attend_block(
        queries[0],
        plane_kv[:, 0],
        frames_near[:, 0::2],
        windows[0],
        row_first,
        col_first,
        frame_here,
        rows_all,
        cols_all,
    )
    return result[None]


def solution(mesh):
    return jax.shard_map(
        local,
        mesh=mesh,
        in_specs=(
            P("ta", "lat", "az", None),
            P(None, "ta", "lat", "az", None),
            P("ta", "lat", "az", None),
        ),
        out_specs=P("ta", "lat", "az", None),
        check_vma=False,
    )
```

profile of v0, /device:TPU:128, one launch (start us, length us, event | category | flops | bytes accessed | tf_op | source)
XLA Modules:
  0.0 206.5 jit_solution(8074772045148341116)
XLA Ops:
  0.0 5.9 %collective-permute-start.1 = (bf16[2,1,16,16,1024]{4,3,2,0,1:T(8,128)(2,1)}, bf16[2,1,16,16,1024]{4,3,2,0,1:T(8,128)(2,1)S(1)}, u32[]{:S(2)}, u32[]{:S(2)}) collective-permute-start(bf16[2,1,16,16,1024]{4,3,2,0,1:T(8,128)(2,1)} %bitcast.111), channel_id=1, source_target_pairs={{32,0},{64,32},{96,64},{128,96},{160,128},{192,160},{224,192},{256... | collective-permute-start | bytes 3145736 | tf_op jit(solution)/shard_map/ppermute | solution.py:22
  5.9 1.9 collective-permute-start
  7.8 21.6 %collective-permute-done.1 = bf16[2,1,16,16,1024]{4,3,2,0,1:T(8,128)(2,1)S(1)} collective-permute-done((bf16[2,1,16,16,1024]{4,3,2,0,1:T(8,128)(2,1)}, bf16[2,1,16,16,1024]{4,3,2,0,1:T(8,128)(2,1)S(1)}, u32[]{:S(2)}, u32[]{:S(2)}) %collective-permute-start.1) | collective-permute-done | bytes 1048608 | tf_op jit(solution)/shard_map/ppermute | solution.py:22
  29.5 1.2 collective-permute-done
  30.7 3.2 %pad_maximum_fusion.1 = bf16[2,1,16,48,1024]{4,3,2,0,1:T(8,128)(2,1)} fusion(bf16[2,1,16,16,1024]{4,3,2,0,1:T(8,128)(2,1)S(1)} %collective-permute-done.1, bf16[2,1,16,16,1024]{4,3,2,0,1:T(8,128)(2,1)} %bitcast.113, bf16[2,1,16,16,1024]{4,3,2,0,1:T(8,128)(2,1)S(1)} %collective-permute-done), kind=kLoop, calls=%fused_computation.47 | loop fusion | flops 9437184 | bytes 6291456 | tf_op jit(solution)/shard_map/concatenate | solution.py:18
  33.9 5.5 %collective-permute-start.3 = (bf16[2,1,16,48,1024]{4,3,2,0,1:T(8,128)(2,1)}, bf16[2,1,16,48,1024]{4,3,2,0,1:T(8,128)(2,1)}, u32[]{:S(2)}, u32[]{:S(2)}) collective-permute-start(bf16[2,1,16,48,1024]{4,3,2,0,1:T(8,128)(2,1)} %pad_maximum_fusion.1), channel_id=1, source_target_pairs={{4,0},{8,4},{12,8},{16,12},{20,16},{24,20},{28,24},{0,28},{5,1},{9... | collective-permute-start | bytes 9437192 | tf_op jit(solution)/shard_map/ppermute | solution.py:22
  39.4 1.9 collective-permute-start.2
  41.4 1.9 collective-permute-start.5
  43.3 6.4 %collective-permute-start.4 = (bf16[2,1,16,16,1024]{4,3,2,1,0:T(8,128)(2,1)}, bf16[2,1,16,16,1024]{4,3,2,1,0:T(8,128)(2,1)S(1)}, u32[]{:S(2)}, u32[]{:S(2)}) collective-permute-start(bf16[2,1,16,16,1024]{4,3,2,1,0:T(8,128)(2,1)} %param.4), channel_id=1, source_target_pairs={{0,1},{1,2},{2,3},{4,5},{5,6},{6,7},{8,9},{9,10},{10,11},{12,13},{... | collective-permute-start | bytes 3145736 | tf_op jit(solution)/shard_map/ppermute | solution.py:20
  51.3 1.9 copy.13
  53.3 38.5 %collective-permute-done.5 = bf16[2,1,16,16,1024]{4,3,2,1,0:T(8,128)(2,1)S(1)} collective-permute-done((bf16[2,1,16,16,1024]{4,3,2,1,0:T(8,128)(2,1)}, bf16[2,1,16,16,1024]{4,3,2,1,0:T(8,128)(2,1)S(1)}, u32[]{:S(2)}, u32[]{:S(2)}) %collective-permute-start.5) | collective-permute-done | bytes 1048608 | tf_op jit(solution)/shard_map/ppermute | solution.py:22
  92.2 1.6 pad_maximum_fusion.2
  94.2 11.7 %collective-permute-done.3 = bf16[2,1,16,48,1024]{4,3,2,0,1:T(8,128)(2,1)} collective-permute-done((bf16[2,1,16,48,1024]{4,3,2,0,1:T(8,128)(2,1)}, bf16[2,1,16,48,1024]{4,3,2,0,1:T(8,128)(2,1)}, u32[]{:S(2)}, u32[]{:S(2)}) %collective-permute-start.3) | collective-permute-done | bytes 3145760 | tf_op jit(solution)/shard_map/ppermute | solution.py:22
  105.9 5.3 %collective-permute-done.2 = bf16[2,1,16,48,1024]{4,3,2,0,1:T(8,128)(2,1)} collective-permute-done((bf16[2,1,16,48,1024]{4,3,2,0,1:T(8,128)(2,1)}, bf16[2,1,16,48,1024]{4,3,2,0,1:T(8,128)(2,1)}, u32[]{:S(2)}, u32[]{:S(2)}) %collective-permute-start.2) | collective-permute-done | bytes 3145760 | tf_op jit(solution)/shard_map/ppermute | solution.py:20
  111.2 7.0 %pad_maximum_fusion = bf16[2,1,48,48,1024]{4,3,2,0,1:T(8,128)(2,1)} fusion(bf16[2,1,16,48,1024]{4,3,2,0,1:T(8,128)(2,1)} %collective-permute-done.3, bf16[2,1,16,16,1024]{4,3,2,0,1:T(8,128)(2,1)S(1)} %copy-done.5, bf16[2,1,16,16,1024]{4,3,2,0,1:T(8,128)(2,1)S(1)} %bitcast.114, bf16[2,1,16,16,1024]{4,3,2,0,1:T(8,128)(2,1)S(1)} %copy-done.7, ...), kind=kLoop, calls=%fused_computation.31 | loop fusion | flops 47185920 | bytes 18874368 | tf_op jit(solution)/shard_map/concatenate | solution.py:18
  118.2 9.0 %copy.11 = bf16[2,6,6,8,8,1024]{5,4,3,2,1,0:T(8,128)(2,1)} copy(bf16[2,6,6,8,8,1024]{5,4,2,3,1,0:T(8,128)(2,1)} %bitcast.108) | data formatting | bytes 18874368 | tf_op jit(solution)/shard_map/transpose | solution.py:41
  127.1 4.9 %fusion.78 = (bf16[44,64,128]{2,1,0:T(8,128)(2,1)}, bf16[44,64,128]{2,1,0:T(8,128)(2,1)}, bf16[44,64,128]{2,1,0:T(8,128)(2,1)}, bf16[44,64,128]{2,1,0:T(8,128)(2...) fusion(bf16[2,8,64,1024]{3,2,1,0:T(8,128)(2,1)S(1)} %bitcast.10, ...), kind=kLoop, calls=%fused_computation.152 | loop fusion | flops 3244032 | bytes 18022400 | tf_op jit(solution)/shard_map/squeeze | solution.py:100
  132.0 0.7 slice-done
  132.8 1.4 slice-done.1
  134.4 3.0 %fusion.63 = (bf16[44,64,128]{2,1,0:T(8,128)(2,1)}, bf16[44,64,128]{2,1,0:T(8,128)(2,1)}, bf16[44,64,128]{2,1,0:T(8,128)(2,1)}, bf16[44,64,128]{2,1,0:T(8,128)(2...) fusion(bf16[2,8,64,1024]{3,2,1,0:T(8,128)(2,1)S(1)} %bitcast.110, ...), kind=kLoop, calls=%fused_computation.137 | loop fusion | flops 10092544 | bytes 16580608 | tf_op jit(solution)/shard_map/squeeze | solution.py:101
  137.3 2.8 %gather_fusion.1 = bf16[60,64,128]{2,1,0:T(8,128)(2,1)} fusion(bf16[44,64,128]{2,1,0:T(8,128)(2,1)} %get-tuple-element.7, s32[1024]{0:T(1024)S(1)} %pad_clamp_fusion), kind=kCustom, calls=%fused_computation.1 | custom fusion | bytes 1966320 | tf_op jit(solution)/shard_map/gather | solution.py:101
  140.1 1.8 gather_fusion
  142.0 2.7 %gather_fusion.3 = bf16[60,64,128]{2,1,0:T(8,128)(2,1)} fusion(bf16[44,64,128]{2,1,0:T(8,128)(2,1)} %get-tuple-element.9, s32[1024]{0:T(1024)S(1)} %pad_clamp_fusion), kind=kCustom, calls=%fused_computation.3 | custom fusion | bytes 1966320 | tf_op jit(solution)/shard_map/gather | solution.py:101
  144.7 2.8 %gather_fusion.2 = bf16[60,64,128]{2,1,0:T(8,128)(2,1)} fusion(bf16[44,64,128]{2,1,0:T(8,128)(2,1)} %get-tuple-element.8, s32[1024]{0:T(1024)S(1)} %pad_clamp_fusion), kind=kCustom, calls=%fused_computation.2 | custom fusion | bytes 1966320 | tf_op jit(solution)/shard_map/gather | solution.py:100
  147.5 2.9 %fusion.113 = (f32[4,64]{1,0:T(4,128)}, f32[4,64,960]{2,1,0:T(8,128)}) fusion(bf16[4,960,128]{2,1,0:T(8,128)(2,1)S(1)} %bitcast.116, bf16[4,64,1024]{2,1,0:T(8,128)(2,1)} %bitcast.132, pred[4,960]{1,0:T(4,128)(4,1)S(1)} %broadcast_in_dim.47), kind=kOutput, calls=%fused_computation.200 | convolution fusion | flops 63651584 | bytes 2036480 | tf_op jit(solution)/shard_map/tqd,tkd->tqk/dot_general | solution.py:103
  150.4 1.8 fusion.114
  152.2 2.7 %gather_fusion.5 = bf16[60,64,128]{2,1,0:T(8,128)(2,1)} fusion(bf16[44,64,128]{2,1,0:T(8,128)(2,1)} %get-tuple-element.11, s32[1024]{0:T(1024)S(1)} %pad_clamp_fusion), kind=kCustom, calls=%fused_computation.5 | custom fusion | bytes 1966320 | tf_op jit(solution)/shard_map/gather | solution.py:101
  154.9 1.7 gather_fusion.4
  156.6 1.8 fusion.115
  158.4 1.6 gather_fusion.7
  160.0 1.7 gather_fusion.6
  161.7 1.8 fusion.116
  163.5 2.8 %gather_fusion.9 = bf16[60,64,128]{2,1,0:T(8,128)(2,1)} fusion(bf16[44,64,128]{2,1,0:T(8,128)(2,1)} %get-tuple-element.16, s32[1024]{0:T(1024)S(1)} %pad_clamp_fusion), kind=kCustom, calls=%fused_computation.9 | custom fusion | bytes 1966320 | tf_op jit(solution)/shard_map/gather | solution.py:101
  166.3 2.8 %gather_fusion.8 = bf16[60,64,128]{2,1,0:T(8,128)(2,1)} fusion(bf16[44,64,128]{2,1,0:T(8,128)(2,1)} %get-tuple-element.15, s32[1024]{0:T(1024)S(1)} %pad_clamp_fusion), kind=kCustom, calls=%fused_computation.8 | custom fusion | bytes 1966320 | tf_op jit(solution)/shard_map/gather | solution.py:100
  169.0 2.7 %fusion.117 = (f32[4,64]{1,0:T(4,128)S(1)}, f32[4,64,960]{2,1,0:T(8,128)}) fusion(bf16[4,960,128]{2,1,0:T(8,128)(2,1)} %bitcast.121, bf16[4,64,1024]{2,1,0:T(8,128)(2,1)} %bitcast.136, pred[4,960]{1,0:T(4,128)(4,1)S(1)} %broadcast_in_dim.47), kind=kOutput, calls=%fused_computation.204 | convolution fusion | flops 63651584 | bytes 2036480 | tf_op jit(solution)/shard_map/tqd,tkd->tqk/dot_general | solution.py:103
  171.8 2.7 %gather_fusion.11 = bf16[60,64,128]{2,1,0:T(8,128)(2,1)} fusion(bf16[44,64,128]{2,1,0:T(8,128)(2,1)} %get-tuple-element.18, s32[1024]{0:T(1024)S(1)} %pad_clamp_fusion), kind=kCustom, calls=%fused_computation.11 | custom fusion | bytes 1966320 | tf_op jit(solution)/shard_map/gather | solution.py:101
  174.5 2.7 %gather_fusion.10 = bf16[60,64,128]{2,1,0:T(8,128)(2,1)} fusion(bf16[44,64,128]{2,1,0:T(8,128)(2,1)} %get-tuple-element.17, s32[1024]{0:T(1024)S(1)} %pad_clamp_fusion), kind=kCustom, calls=%fused_computation.10 | custom fusion | bytes 1966320 | tf_op jit(solution)/shard_map/gather | solution.py:100
  177.3 2.7 %fusion.118 = (f32[4,64]{1,0:T(4,128)S(1)}, f32[4,64,960]{2,1,0:T(8,128)}) fusion(bf16[4,960,128]{2,1,0:T(8,128)(2,1)} %bitcast.122, bf16[4,64,1024]{2,1,0:T(8,128)(2,1)} %bitcast.137, pred[4,960]{1,0:T(4,128)(4,1)S(1)} %broadcast_in_dim.47), kind=kOutput, calls=%fused_computation.205 | convolution fusion | flops 63651584 | bytes 2036480 | tf_op jit(solution)/shard_map/tqd,tkd->tqk/dot_general | solution.py:103
  179.9 2.7 %gather_fusion.13 = bf16[60,64,128]{2,1,0:T(8,128)(2,1)} fusion(bf16[44,64,128]{2,1,0:T(8,128)(2,1)} %get-tuple-element.20, s32[1024]{0:T(1024)S(1)} %pad_clamp_fusion), kind=kCustom, calls=%fused_computation.13 | custom fusion | bytes 1966320 | tf_op jit(solution)/shard_map/gather | solution.py:101
  182.7 2.7 %gather_fusion.12 = bf16[60,64,128]{2,1,0:T(8,128)(2,1)} fusion(bf16[44,64,128]{2,1,0:T(8,128)(2,1)} %get-tuple-element.19, s32[1024]{0:T(1024)S(1)} %pad_clamp_fusion), kind=kCustom, calls=%fused_computation.12 | custom fusion | bytes 1966320 | tf_op jit(solution)/shard_map/gather | solution.py:100
  185.4 2.7 %fusion.119 = (f32[4,64]{1,0:T(4,128)S(1)}, f32[4,64,960]{2,1,0:T(8,128)}) fusion(bf16[4,960,128]{2,1,0:T(8,128)(2,1)} %bitcast.123, bf16[4,64,1024]{2,1,0:T(8,128)(2,1)} %bitcast.138, pred[4,960]{1,0:T(4,128)(4,1)S(1)} %broadcast_in_dim.47), kind=kOutput, calls=%fused_computation.206 | convolution fusion | flops 63651584 | bytes 2036480 | tf_op jit(solution)/shard_map/tqd,tkd->tqk/dot_general | solution.py:103
  188.1 2.7 %gather_fusion.15 = bf16[60,64,128]{2,1,0:T(8,128)(2,1)} fusion(bf16[44,64,128]{2,1,0:T(8,128)(2,1)} %get-tuple-element.14, s32[1024]{0:T(1024)S(1)} %pad_clamp_fusion), kind=kCustom, calls=%fused_computation.15 | custom fusion | bytes 1966320 | tf_op jit(solution)/shard_map/gather | solution.py:101
  190.8 2.7 %gather_fusion.14 = bf16[60,64,128]{2,1,0:T(8,128)(2,1)} fusion(bf16[44,64,128]{2,1,0:T(8,128)(2,1)} %get-tuple-element.5, s32[1024]{0:T(1024)S(1)} %pad_clamp_fusion), kind=kCustom, calls=%fused_computation.14 | custom fusion | bytes 1966320 | tf_op jit(solution)/shard_map/gather | solution.py:100
  193.6 1.9 fusion.120
  195.6 2.0 fusion.32
  197.5 1.9 fusion.17
  200.4 1.5 fusion.40
  205.6 0.8 copy.14
  (66 shorter events, 7.3 us)
Async XLA Ops:
  0.0 29.5 %collective-permute-start.1 = (bf16[2,1,16,16,1024]{4,3,2,0,1:T(8,128)(2,1)}, bf16[2,1,16,16,1024]{4,3,2,0,1:T(8,128)(2,1)S(1)}, u32[]{:S(2)}, u32[]{:S(2)}) collective-permute-start(bf16[2,1,16,16,1024]{4,3,2,0,1:T(8,128)(2,1)} %bitcast.111), channel_id=1, source_target_pairs={{32,0},{64,32},{96,64},{128,96},{160,128},{192,160},{224,192},{256... | collective-permute-start | bytes 3145736 | tf_op jit(solution)/shard_map/ppermute | solution.py:22
  5.9 24.8 %collective-permute-start = (bf16[2,1,16,16,1024]{4,3,2,0,1:T(8,128)(2,1)}, bf16[2,1,16,16,1024]{4,3,2,0,1:T(8,128)(2,1)S(1)}, u32[]{:S(2)}, u32[]{:S(2)}) collective-permute-start(bf16[2,1,16,16,1024]{4,3,2,0,1:T(8,128)(2,1)} %bitcast.112), channel_id=1, source_target_pairs={{0,32},{32,64},{64,96},{96,128},{128,160},{160,192},{192,224},{224... | collective-permute-start | bytes 3145736 | tf_op jit(solution)/shard_map/ppermute | solution.py:20
  29.5 1.2 copy-start.4
  30.7 3.2 %copy-start.6 = (bf16[2,1,16,16,1024]{4,3,2,0,1:T(8,128)(2,1)}, bf16[2,1,16,16,1024]{4,3,2,0,1:T(8,128)(2,1)S(1)}, u32[]{:S(2)}) copy-start(bf16[2,1,16,16,1024]{4,3,2,0,1:T(8,128)(2,1)S(1)} %collective-permute-done) | copy-start | bytes 3145732
  33.9 77.3 %copy-start.3 = (bf16[2,1,16,16,1024]{4,3,2,1,0:T(8,128)(2,1)S(1)}, bf16[2,1,16,16,1024]{4,3,2,1,0:T(8,128)(2,1)}, u32[]{:S(2)}) copy-start(bf16[2,1,16,16,1024]{4,3,2,1,0:T(8,128)(2,1)} %param.4) | copy-start | bytes 3145732
  33.9 72.0 %collective-permute-start.3 = (bf16[2,1,16,48,1024]{4,3,2,0,1:T(8,128)(2,1)}, bf16[2,1,16,48,1024]{4,3,2,0,1:T(8,128)(2,1)}, u32[]{:S(2)}, u32[]{:S(2)}) collective-permute-start(bf16[2,1,16,48,1024]{4,3,2,0,1:T(8,128)(2,1)} %pad_maximum_fusion.1), channel_id=1, source_target_pairs={{4,0},{8,4},{12,8},{16,12},{20,16},{24,20},{28,24},{0,28},{5,1},{9... | collective-permute-start | bytes 9437192 | tf_op jit(solution)/shard_map/ppermute | solution.py:22
  39.4 71.8 %collective-permute-start.2 = (bf16[2,1,16,48,1024]{4,3,2,0,1:T(8,128)(2,1)}, bf16[2,1,16,48,1024]{4,3,2,0,1:T(8,128)(2,1)}, u32[]{:S(2)}, u32[]{:S(2)}) collective-permute-start(bf16[2,1,16,48,1024]{4,3,2,0,1:T(8,128)(2,1)} %pad_maximum_fusion.1), channel_id=1, source_target_pairs={{0,4},{4,8},{8,12},{12,16},{16,20},{20,24},{24,28},{28,0},{1,5},{5... | collective-permute-start | bytes 9437192 | tf_op jit(solution)/shard_map/ppermute | solution.py:20
  41.4 50.5 %collective-permute-start.5 = (bf16[2,1,16,16,1024]{4,3,2,1,0:T(8,128)(2,1)}, bf16[2,1,16,16,1024]{4,3,2,1,0:T(8,128)(2,1)S(1)}, u32[]{:S(2)}, u32[]{:S(2)}) collective-permute-start(bf16[2,1,16,16,1024]{4,3,2,1,0:T(8,128)(2,1)} %param.4), channel_id=1, source_target_pairs={{1,0},{2,1},{3,2},{5,4},{6,5},{7,6},{9,8},{10,9},{11,10},{13,12},{... | collective-permute-start | bytes 3145736 | tf_op jit(solution)/shard_map/ppermute | solution.py:22
  43.3 48.9 %collective-permute-start.4 = (bf16[2,1,16,16,1024]{4,3,2,1,0:T(8,128)(2,1)}, bf16[2,1,16,16,1024]{4,3,2,1,0:T(8,128)(2,1)S(1)}, u32[]{:S(2)}, u32[]{:S(2)}) collective-permute-start(bf16[2,1,16,16,1024]{4,3,2,1,0:T(8,128)(2,1)} %param.4), channel_id=1, source_target_pairs={{0,1},{1,2},{2,3},{4,5},{5,6},{6,7},{8,9},{9,10},{10,11},{12,13},{... | collective-permute-start | bytes 3145736 | tf_op jit(solution)/shard_map/ppermute | solution.py:20
  53.3 57.9 %copy-start.5 = (bf16[2,1,16,16,1024]{4,3,2,0,1:T(8,128)(2,1)S(1)}, bf16[2,1,16,16,1024]{4,3,2,0,1:T(8,128)(2,1)}, u32[]{:S(2)}) copy-start(bf16[2,1,16,16,1024]{4,3,2,0,1:T(8,128)(2,1)} %copy-done.4) | copy-start | bytes 3145732
  53.3 57.9 %copy-start.7 = (bf16[2,1,16,16,1024]{4,3,2,0,1:T(8,128)(2,1)S(1)}, bf16[2,1,16,16,1024]{4,3,2,0,1:T(8,128)(2,1)}, u32[]{:S(2)}) copy-start(bf16[2,1,16,16,1024]{4,3,2,0,1:T(8,128)(2,1)} %copy-done.6) | copy-start | bytes 3145732
  127.1 5.6 %slice-start = ((s8[9437184]{0:T(1024)(128)(4,1)}), s8[4194304]{0:T(1024)(128)(4,1)S(1)}, s32[]{:S(2)}) async-start(s8[9437184]{0:T(1024)(128)(4,1)} %bitcast.105), calls=%async_computation | async-start | bytes 8388608
  127.1 7.0 %slice-start.1 = ((s8[9437184]{0:T(1024)(128)(4,1)}), s8[4194304]{0:T(1024)(128)(4,1)S(1)}, s32[]{:S(2)}) async-start(s8[9437184]{0:T(1024)(128)(4,1)} %bitcast.105), calls=%async_computation.1 | async-start | bytes 8388608
  127.1 7.2 %slice-start.2 = ((s8[9437184]{0:T(1024)(128)(4,1)}), s8[1048576]{0:T(1024)(128)(4,1)S(1)}, s32[]{:S(2)}) async-start(s8[9437184]{0:T(1024)(128)(4,1)} %bitcast.105), calls=%async_computation.2 | async-start | bytes 2097152
  137.3 17.6 %copy-start.8 = (bf16[44,64,128]{2,1,0:T(8,128)(2,1)S(1)}, bf16[44,64,128]{2,1,0:T(8,128)(2,1)}, u32[]{:S(2)}) copy-start(bf16[44,64,128]{2,1,0:T(8,128)(2,1)} %get-tuple-element.10) | copy-start | bytes 2162692
  171.8 23.8 %copy-start.16 = (f32[4,64]{1,0:T(4,128)S(1)}, f32[4,64]{1,0:T(4,128)}, u32[]{:S(2)}) copy-start(f32[4,64]{1,0:T(4,128)} %get-tuple-element.27) | copy-start | bytes 3076
  193.6 8.3 %copy-start.1 = (f32[4,64,960]{2,1,0:T(8,128)S(1)}, f32[4,64,960]{2,1,0:T(8,128)}, u32[]{:S(2)}) copy-start(f32[4,64,960]{2,1,0:T(8,128)} %get-tuple-element.38) | copy-start | bytes 2949124
  193.6 8.6 %copy-start.2 = (f32[4,64,960]{2,1,0:T(8,128)S(1)}, f32[4,64,960]{2,1,0:T(8,128)}, u32[]{:S(2)}) copy-start(f32[4,64,960]{2,1,0:T(8,128)} %get-tuple-element.40) | copy-start | bytes 2949124
  193.6 9.2 %copy-start.9 = (bf16[60,64,128]{2,1,0:T(8,128)(2,1)S(1)}, bf16[60,64,128]{2,1,0:T(8,128)(2,1)}, u32[]{:S(2)}) copy-start(bf16[60,64,128]{2,1,0:T(8,128)(2,1)} %gather_fusion.3) | copy-start | bytes 2949124
  193.6 9.6 %copy-start.10 = (bf16[60,64,128]{2,1,0:T(8,128)(2,1)S(1)}, bf16[60,64,128]{2,1,0:T(8,128)(2,1)}, u32[]{:S(2)}) copy-start(bf16[60,64,128]{2,1,0:T(8,128)(2,1)} %gather_fusion.5) | copy-start | bytes 2949124
  193.6 10.0 %copy-start.11 = (bf16[60,64,128]{2,1,0:T(8,128)(2,1)S(1)}, bf16[60,64,128]{2,1,0:T(8,128)(2,1)}, u32[]{:S(2)}) copy-start(bf16[60,64,128]{2,1,0:T(8,128)(2,1)} %gather_fusion.7) | copy-start | bytes 2949124
  193.6 10.4 %copy-start = (f32[4,64,960]{2,1,0:T(8,128)S(1)}, f32[4,64,960]{2,1,0:T(8,128)}, u32[]{:S(2)}) copy-start(f32[4,64,960]{2,1,0:T(8,128)} %get-tuple-element.36) | copy-start | bytes 2949124
  193.6 10.4 %copy-start.12 = (bf16[60,64,128]{2,1,0:T(8,128)(2,1)S(1)}, bf16[60,64,128]{2,1,0:T(8,128)(2,1)}, u32[]{:S(2)}) copy-start(bf16[60,64,128]{2,1,0:T(8,128)(2,1)} %gather_fusion.9) | copy-start | bytes 2949124
  195.6 8.9 %copy-start.13 = (bf16[60,64,128]{2,1,0:T(8,128)(2,1)S(1)}, bf16[60,64,128]{2,1,0:T(8,128)(2,1)}, u32[]{:S(2)}) copy-start(bf16[60,64,128]{2,1,0:T(8,128)(2,1)} %gather_fusion.11) | copy-start | bytes 2949124
  199.4 5.4 %copy-start.14 = (bf16[60,64,128]{2,1,0:T(8,128)(2,1)S(1)}, bf16[60,64,128]{2,1,0:T(8,128)(2,1)}, u32[]{:S(2)}) copy-start(bf16[60,64,128]{2,1,0:T(8,128)(2,1)} %gather_fusion.13) | copy-start | bytes 2949124
  199.7 5.5 %copy-start.15 = (bf16[60,64,128]{2,1,0:T(8,128)(2,1)S(1)}, bf16[60,64,128]{2,1,0:T(8,128)(2,1)}, u32[]{:S(2)}) copy-start(bf16[60,64,128]{2,1,0:T(8,128)(2,1)} %gather_fusion.15) | copy-start | bytes 2949124
where the time goes:
time: 208 us; the launch traced here: 206 us
  waiting for transfers between devices  78.8 us (38%)
  local copies, waits for them, and re-layouts  54.7 us (26%)
  other arithmetic  26.3 us (13%)
  starting transfers between devices  23.6 us (11%)
  matrix products  22.9 us (11%)
    ppermute x3, waiting for transfers between devices, extended(): lax.ppermute(head, axis, [((i + 1) % count, i) for i in range(ends)])  71.9 us
    gather x8, local copies, waits for them, and re-layouts, attend_block(): key_pool[1][position].reshape(own_tiles, slot_count * tokens, HD)  21 us
    gather x8, local copies, waits for them, and re-layouts, attend_block(): key_pool[0][position].reshape(own_tiles, slot_count * tokens, HD)  19 us
    dot_general x8, matrix products, attend_block(): jnp.einsum('tqd,tkd->tqk', query_part, key_block, preferred_element_type=...  18.2 us
    ppermute x3, starting transfers between devices, extended(): lax.ppermute(head, axis, [((i + 1) % count, i) for i in range(ends)])  13.3 us
    concatenate x3, other arithmetic, extended(): jnp.concatenate([lax.ppermute(tail, axis, [(i, (i + 1) % count) for i in...  11.7 us
    ppermute x3, starting transfers between devices, extended(): lax.ppermute(tail, axis, [(i, (i + 1) % count) for i in range(ends)])  10.2 us
    transpose x2, local copies, waits for them, and re-layouts, tile_split(): shaped.transpose(axis_order)  9.12 us
  transfers between devices with their start and end apart: 6, of which 6 were waited for; matrix products, arithmetic and copies ran while one was open for 3% of the time, Pallas kernels for 0%

commit v1 on v0

v1 whole, which is shorter than its diff:
```python
import functools
import math

import jax
import jax.numpy as jnp
from jax import lax
from jax.experimental import pallas as pl
from jax.experimental.pallas import tpu as pltpu
from jax.sharding import PartitionSpec as P

MESH = pl.DeviceIdType.MESH
HD = 128
TS = 8
ROWS, COLS = 16, 16
PAIR = TS * COLS
NEG = -1e30

OWN, CORE, CROSS, XREL, TDIR, TREL, UP, DOWN = range(8)
CORNER_UP, CORNER_DOWN = 8, 9
TRANSFERS = (CORE, CROSS, XREL, TDIR, TREL, UP, DOWN, CORNER_UP, CORNER_DOWN)
KEYS, VALUES = 0, 1
CHUNKS = [(kind, half) for kind in (KEYS, VALUES) for half in (0, 1)]

CORNER = 8
PLACES = [
    {
        (OWN, 0): 0, (OWN, 1): 1, (CORE, 0): 2, (CORE, 1): 3, (XREL, 0): 4, (XREL, 1): 5,
        (UP, 0): 6, (UP, 1): 7, (DOWN, 0): 8, (CORNER, 0): 9, (TREL, 0): 10, (TDIR, 0): 11,
    },
    {
        (OWN, 0): 0, (OWN, 1): 1, (CORE, 0): 2, (CORE, 1): 3, (XREL, 0): 4, (XREL, 1): 5,
        (UP, 1): 6, (DOWN, 0): 7, (DOWN, 1): 8, (CORNER, 1): 9, (TREL, 1): 10, (TDIR, 1): 11,
    },
]
NPLACE = 12


def when(condition, action):
    if condition is None:
        action()
    else:
        pl.when(condition)(action)


def kernel(
    heads, n_az, n_lat, n_ta, windows, q_hbm, kv_hbm, out_hbm,
    blocks, corner, corner_out, q, bias, scores, weights, peak, total, acc, out,
    send_sem, recv_sem, local_sem,
):
    az, lat, ta = lax.axis_index("az"), lax.axis_index("lat"), lax.axis_index("ta")
    place4 = lax.rem(az, 4)
    core = lax.rem(az, 2)
    cross = az + 3 - 2 * place4
    step = jnp.where(place4 >= 2, 1, -1)
    x_step = jnp.where(place4 == 3, -4, 4)
    outer = (place4 == 0) | (place4 == 3)
    frame_ok = lambda f: (f >= 0) & (f < n_ta)
    at = lambda a, l, t: {"az": a, "lat": l, "ta": t}
    routes = {
        CORE: (at(az + 1 - 2 * core, lat, ta),) * 2 + (None, None),
        CROSS: (at(cross, lat, ta),) * 2 + (None, None),
        XREL: (
            at(lax.rem(az + x_step + n_az, n_az), lat, ta),
            at(lax.rem(az - x_step + n_az, n_az), lat, ta),
            outer, outer,
        ),
        TDIR: (at(az, lat, ta + step), at(az, lat, ta - step), frame_ok(ta + step), frame_ok(ta - step)),
        TREL: (at(cross, lat, ta + step),) * 2 + (frame_ok(ta + step),) * 2,
        UP: (at(az, lat + 1, ta), at(az, lat - 1, ta), lat < n_lat - 1, lat > 0),
        DOWN: (at(az, lat - 1, ta), at(az, lat + 1, ta), lat > 0, lat < n_lat - 1),
    }
    routes[CORNER_UP] = routes[UP]
    routes[CORNER_DOWN] = routes[DOWN]

    barrier = pltpu.get_barrier_semaphore()
    count = 0
    for name in (CORE, CROSS, XREL, TDIR, TREL, UP, DOWN):
        _, source, sends, receives = routes[name]
        when(receives, functools.partial(
            pl.semaphore_signal, barrier, inc=1, device_id=source, device_id_type=MESH))
        count = count + (1 if sends is None else sends.astype(jnp.int32))
    pl.semaphore_wait(barrier, count)

    def rows(half):
        return pl.ds(half * TS, TS)

    def copy(name, kind, half):
        slot = TRANSFERS.index(name)
        chunk = 2 * kind + half
        if name in (CORNER_UP, CORNER_DOWN):
            source = corner_out.at[name - CORNER_UP, kind]
            target = corner.at[name - CORNER_UP, kind]
        else:
            target = blocks.at[name, kind, rows(half)]
            if name in (XREL, TREL):
                source = blocks.at[CROSS, kind, rows(half)]
            else:
                source = kv_hbm.at[kind, 0, rows(half)]
        return pltpu.make_async_remote_copy(
            src_ref=source, dst_ref=target,
            send_sem=send_sem.at[slot, chunk], recv_sem=recv_sem.at[slot, chunk],
            device_id=routes[name][0], device_id_type=MESH,
        )

    started = []

    def start(name, kind, halves=(0, 1)):
        for half in halves:
            started.append((name, kind, half))
            when(routes[name][2], copy(name, kind, half).start)

    def arrived(name, kind, halves=(0, 1)):
        for half in halves:
            when(routes[name][3], copy(name, kind, half).wait_recv)

    def relay(kind, half):
        arrived(CROSS, kind, (half,))
        start(XREL, kind, (half,))
        start(TREL, kind, (half,))

    start(CROSS, KEYS)
    start(TDIR, KEYS)
    start(UP, KEYS)
    start(DOWN, KEYS)
    start(CORE, KEYS)
    get_q = pltpu.make_async_copy(q_hbm.at[0], q, local_sem.at[0])
    get_k = pltpu.make_async_copy(kv_hbm.at[KEYS, 0], blocks.at[OWN, KEYS], local_sem.at[1])
    get_v = pltpu.make_async_copy(kv_hbm.at[VALUES, 0], blocks.at[OWN, VALUES], local_sem.at[2])
    get_q.start()
    get_k.start()
    get_v.start()
    start(CROSS, VALUES)
    start(CORE, VALUES)
    start(UP, VALUES)
    start(DOWN, VALUES)

    def clear(name):
        def body():
            blocks[name] = jnp.zeros(blocks.shape[1:], blocks.dtype)
        return body

    def clear_corner(index):
        def body():
            corner[index] = jnp.zeros(corner.shape[1:], corner.dtype)
        return body

    for name in (TDIR, TREL, UP, DOWN):
        when(jnp.logical_not(routes[name][3]), clear(name))
    when(lat == 0, clear_corner(0))
    when(lat == n_lat - 1, clear_corner(1))

    rows_all, cols_all = 2 * n_lat, 2 * n_az
    lane = lax.broadcasted_iota(jnp.int32, (8, PAIR), 1)
    right_tile = lax.rem(lane // TS, 2)
    col_on = jnp.where(core == 0, 2, -2)
    for r in range(2):
        tiles = [None] * NPLACE
        for (name, half), place in PLACES[r].items():
            frame, row, col = ta, half, right_tile
            if name == CORE:
                col = col + col_on
            elif name == XREL:
                col = col - col_on
            elif name == UP:
                row = half - 2
            elif name == DOWN:
                row = half + 2
            elif name == CORNER:
                row = 3 * half - 1
                col = jnp.where(right_tile == 0, 2, -1)
            elif name == TDIR:
                frame = ta - step
            elif name == TREL:
                frame = ta + step
            row = row + 2 * lat
            there = (row >= 0) & (row < rows_all) & (frame >= 0) & (frame < n_ta)
            first = jnp.where(there, (frame * rows_all + row) * cols_all, -4 * cols_all)
            tiles[place] = first + lax.rem(col + 2 * az + cols_all, cols_all)
        tiles = jnp.stack(tiles, axis=0)
        for c in range(2):
            listed = tiles == windows[0, r, c, 0]
            for slot in range(1, windows.shape[3]):
                listed = listed | (tiles == windows[0, r, c, slot])
            bias[r, :, c * 8:(c + 1) * 8, :] = jnp.where(listed, 0.0, NEG)

    off = jnp.where(outer, XREL, CROSS)
    scale = 1.0 / math.sqrt(HD)

    def key_block(name, half, kind, columns):
        if name == CORNER:
            block = corner[half, kind, :, :, columns]
        else:
            block = blocks[off if name == XREL else name, kind, rows(half), :, columns]
        return block.reshape(PAIR, HD)

    def add_keys(*names, first=False):
        def head(h, carry):
            columns = pl.ds(pl.multiple_of(h * HD, HD), HD)
            for r in range(2):
                query = q[rows(r), :, columns].reshape(PAIR, HD)
                best = None if first else peak[r, h]
                for (name, half), place in PLACES[r].items():
                    if name not in names:
                        continue
                    score = lax.dot_general(
                        query, key_block(name, half, KEYS, columns), (((1,), (1,)), ((), ())),
                        preferred_element_type=jnp.float32,
                    )
                    score = score.reshape(TS, COLS, PAIR) * scale + bias[r, place][None]
                    score = score.reshape(PAIR, PAIR)
                    scores[r, h, :, place * PAIR:(place + 1) * PAIR] = score
                    best = score if best is None else jnp.maximum(best, score)
                peak[r, h] = best
            return carry
        lax.fori_loop(0, heads, head, 0)

    def softmax():
        def head(h, carry):
            for r in range(2):
                most = jnp.broadcast_to(jnp.max(peak[r, h], axis=-1, keepdims=True), (PAIR, PAIR))
                summed = None
                for place in range(NPLACE):
                    part = slice(place * PAIR, (place + 1) * PAIR)
                    weight = jnp.exp(scores[r, h, :, part] - most)
                    weights[r, h, :, part] = weight.astype(jnp.bfloat16)
                    summed = weight if summed is None else summed + weight
                total[r, h] = jnp.broadcast_to(
                    1.0 / jnp.sum(summed, axis=-1, keepdims=True), (PAIR, PAIR))
            return carry
        lax.fori_loop(0, heads, head, 0)

    def add_values(*names, first=False, last=False):
        def head(h, carry):
            columns = pl.ds(pl.multiple_of(h * HD, HD), HD)
            for r in range(2):
                result = None if first else acc[r, h]
                for (name, half), place in PLACES[r].items():
                    if name not in names:
                        continue
                    part = jnp.dot(
                        weights[r, h, :, place * PAIR:(place + 1) * PAIR],
                        key_block(name, half, VALUES, columns),
                        preferred_element_type=jnp.float32,
                    )
                    result = part if result is None else result + part
                if last:
                    result = (result * total[r, h]).astype(jnp.bfloat16)
                    out[rows(r), :, columns] = result.reshape(TS, COLS, HD)
                else:
                    acc[r, h] = result
            return carry
        lax.fori_loop(0, heads, head, 0)

    left_half = lax.broadcasted_iota(jnp.int32, (TS, COLS, heads * HD), 1) < TS

    def send_corners(kind):
        from_on = left_half == (core == 0)
        for index, half in ((0, 1), (1, 0)):
            on = blocks[CORE, kind, rows(half)]
            beyond = blocks[off, kind, rows(half)]
            corner_out[index, kind] = jnp.where(from_on, on, beyond)
        start(CORNER_UP, kind, (0,))
        start(CORNER_DOWN, kind, (0,))

    get_q.wait()
    get_k.wait()
    add_keys(OWN, first=True)
    arrived(CORE, KEYS)
    add_keys(CORE)
    relay(KEYS, 0)
    start(TDIR, VALUES, (0,))
    relay(KEYS, 1)
    start(TDIR, VALUES, (1,))
    arrived(UP, KEYS)
    arrived(DOWN, KEYS)
    add_keys(UP, DOWN)
    arrived(XREL, KEYS)
    send_corners(KEYS)
    add_keys(XREL)
    relay(VALUES, 0)
    arrived(TDIR, KEYS)
    arrived(TREL, KEYS)
    add_keys(TDIR, TREL)
    arrived(CORNER_UP, KEYS, (0,))
    arrived(CORNER_DOWN, KEYS, (0,))
    add_keys(CORNER)
    relay(VALUES, 1)
    softmax()
    arrived(CORE, VALUES)
    arrived(XREL, VALUES)
    send_corners(VALUES)
    arrived(UP, VALUES)
    arrived(DOWN, VALUES)
    get_v.wait()
    add_values(OWN, CORE, XREL, UP, DOWN, first=True)
    arrived(CORNER_UP, VALUES, (0,))
    arrived(CORNER_DOWN, VALUES, (0,))
    arrived(TREL, VALUES)
    arrived(TDIR, VALUES)
    add_values(CORNER, TREL, TDIR, last=True)
    put = pltpu.make_async_copy(out, out_hbm.at[0], local_sem.at[0])
    put.start()
    for name, kind, half in started:
        when(routes[name][2], copy(name, kind, half).wait_send)
    put.wait()


def solution(mesh):
    n_az, n_lat, n_ta = mesh.shape["az"], mesh.shape["lat"], mesh.shape["ta"]

    def local(queries, keys_values, windows):
        width = queries.shape[-1]
        heads = width // HD
        vmem = pltpu.VMEM
        return pl.pallas_call(
            functools.partial(kernel, heads, n_az, n_lat, n_ta),
            out_shape=jax.ShapeDtypeStruct(queries.shape, queries.dtype),
            in_specs=[
                pl.BlockSpec(memory_space=pltpu.SMEM),
                pl.BlockSpec(memory_space=pl.ANY),
                pl.BlockSpec(memory_space=pl.ANY),
            ],
            out_specs=pl.BlockSpec(memory_space=pl.ANY),
            scratch_shapes=[
                vmem((8, 2, ROWS, COLS, width), jnp.bfloat16),
                vmem((2, 2, TS, COLS, width), jnp.bfloat16),
                vmem((2, 2, TS, COLS, width), jnp.bfloat16),
                vmem((ROWS, COLS, width), jnp.bfloat16),
                vmem((2, NPLACE, 16, PAIR), jnp.float32),
                vmem((2, heads, PAIR, NPLACE * PAIR), jnp.float32),
                vmem((2, heads, PAIR, NPLACE * PAIR), jnp.bfloat16),
                vmem((2, heads, PAIR, PAIR), jnp.float32),
                vmem((2, heads, PAIR, PAIR), jnp.float32),
                vmem((2, heads, PAIR, HD), jnp.float32),
                vmem((ROWS, COLS, width), jnp.bfloat16),
                pltpu.SemaphoreType.DMA((len(TRANSFERS), 4)),
                pltpu.SemaphoreType.DMA((len(TRANSFERS), 4)),
                pltpu.SemaphoreType.DMA((3,)),
            ],
            compiler_params=pltpu.CompilerParams(
                collective_id=0, has_side_effects=True, vmem_limit_bytes=56 * 2**20),
            name="tile_attention",
        )(windows, queries, keys_values)

    return jax.shard_map(
        local,
        mesh=mesh,
        in_specs=(
            P("ta", "lat", "az", None),
            P(None, "ta", "lat", "az", None),
            P("ta", "lat", "az", None),
        ),
        out_specs=P("ta", "lat", "az", None),
        check_vma=False,
    )
```

time: 208 us -> 72.7 us (0.35)
  the two profiles are of different devices: /device:TPU:128 before, /device:TPU:152 now
where the time goes in v1:
time: 72.7 us; the launch traced here: 72.5 us
  Pallas kernels  70.6 us (97%)
  local copies, waits for them, and re-layouts  1.88 us (3%)
    pallas_call x1, Pallas kernels, local(): pl.pallas_call(functools.partial(kernel, heads, n_az, n_lat, n_ta), out_s...  70.6 us
    unnamed x1, local copies, waits for them, and re-layouts  1.88 us

profile of v1, /device:TPU:152, one launch (start us, length us, event | category | flops | bytes accessed | tf_op | source)
XLA Modules:
  0.0 72.5 jit_solution(6202604738514936205)
XLA Ops:
  0.0 70.6 %tile_attention.1 = bf16[1,16,16,1024]{3,2,1,0:T(8,128)(2,1)} custom-call(s32[1,2,2,15]{3,2,1,0:T(2,128)} %windows.1, bf16[1,16,16,1024]{3,2,1,0:T(8,128)(2,1)} %q_hbm.1, bf16[2,1,16,16,1024]{4,3,2,1,0:T(8,128)(2,1)} %kv_hbm.1), custom_call_target="tpu_custom_call" | custom-call | tf_op jit(solution)/shard_map/tile_attention/pallas_call | solution.py:315
  70.6 1.9 %copy.5 = bf16[1,16,16,1024]{3,2,1,0:T(8,128)(2,1)} copy(bf16[1,16,16,1024]{3,2,1,0:T(8,128)(2,1)} %tile_attention.1) | data formatting | bytes 1048576

commit v2 on v1

--- a/solution.py
+++ b/solution.py
@@ -17,9 +17,10 @@
 
 OWN, CORE, CROSS, XREL, TDIR, TREL, UP, DOWN = range(8)
 CORNER_UP, CORNER_DOWN = 8, 9
+PIECEWISE = (CROSS, XREL, TDIR, TREL)
 TRANSFERS = (CORE, CROSS, XREL, TDIR, TREL, UP, DOWN, CORNER_UP, CORNER_DOWN)
 KEYS, VALUES = 0, 1
-CHUNKS = [(kind, half) for kind in (KEYS, VALUES) for half in (0, 1)]
+QUARTER = ROWS // 4
 
 CORNER = 8
 PLACES = [
@@ -43,9 +44,9 @@
 
 
 def kernel(
-    heads, n_az, n_lat, n_ta, windows, q_hbm, kv_hbm, out_hbm,
+    heads, n_az, n_lat, n_ta, windows_hbm, q_hbm, kv_hbm, out_hbm,
     blocks, corner, corner_out, q, bias, scores, weights, peak, total, acc, out,
-    send_sem, recv_sem, local_sem,
+    windows, send_sem, recv_sem, local_sem,
 ):
     az, lat, ta = lax.axis_index("az"), lax.axis_index("lat"), lax.axis_index("ta")
     place4 = lax.rem(az, 4)
@@ -84,18 +85,19 @@
     def rows(half):
         return pl.ds(half * TS, TS)
 
-    def copy(name, kind, half):
+    def copy(name, kind, piece):
         slot = TRANSFERS.index(name)
-        chunk = 2 * kind + half
+        chunk = 4 * kind + piece
         if name in (CORNER_UP, CORNER_DOWN):
             source = corner_out.at[name - CORNER_UP, kind]
             target = corner.at[name - CORNER_UP, kind]
         else:
-            target = blocks.at[name, kind, rows(half)]
+            part = pl.ds(piece * QUARTER, QUARTER) if name in PIECEWISE else pl.ds(0, ROWS)
+            target = blocks.at[name, kind, part]
             if name in (XREL, TREL):
-                source = blocks.at[CROSS, kind, rows(half)]
+                source = blocks.at[CROSS, kind, part]
             else:
-                source = kv_hbm.at[kind, 0, rows(half)]
+                source = kv_hbm.at[kind, 0, part]
         return pltpu.make_async_remote_copy(
             src_ref=source, dst_ref=target,
             send_sem=send_sem.at[slot, chunk], recv_sem=recv_sem.at[slot, chunk],
@@ -104,32 +106,37 @@
 
     started = []
 
-    def start(name, kind, halves=(0, 1)):
-        for half in halves:
-            started.append((name, kind, half))
-            when(routes[name][2], copy(name, kind, half).start)
-
-    def arrived(name, kind, halves=(0, 1)):
-        for half in halves:
-            when(routes[name][3], copy(name, kind, half).wait_recv)
-
-    def relay(kind, half):
-        arrived(CROSS, kind, (half,))
-        start(XREL, kind, (half,))
-        start(TREL, kind, (half,))
+    def pieces(name):
+        return range(4) if name in PIECEWISE else range(1)
+
+    def start(name, kind, some=None):
+        for piece in pieces(name) if some is None else some:
+            started.append((name, kind, piece))
+            when(routes[name][2], copy(name, kind, piece).start)
+
+    def arrived(name, kind, some=None):
+        for piece in pieces(name) if some is None else some:
+            when(routes[name][3], copy(name, kind, piece).wait_recv)
+
+    def relay(kind, piece):
+        arrived(CROSS, kind, (piece,))
+        start(XREL, kind, (piece,))
+        start(TREL, kind, (piece,))
+        start(TDIR, kind, (piece,))
 
     start(CROSS, KEYS)
-    start(TDIR, KEYS)
+    start(CROSS, VALUES)
     start(UP, KEYS)
     start(DOWN, KEYS)
     start(CORE, KEYS)
+    get_windows = pltpu.make_async_copy(windows_hbm, windows, local_sem.at[3])
+    get_windows.start()
     get_q = pltpu.make_async_copy(q_hbm.at[0], q, local_sem.at[0])
     get_k = pltpu.make_async_copy(kv_hbm.at[KEYS, 0], blocks.at[OWN, KEYS], local_sem.at[1])
     get_v = pltpu.make_async_copy(kv_hbm.at[VALUES, 0], blocks.at[OWN, VALUES], local_sem.at[2])
     get_q.start()
     get_k.start()
     get_v.start()
-    start(CROSS, VALUES)
     start(CORE, VALUES)
     start(UP, VALUES)
     start(DOWN, VALUES)
@@ -149,6 +156,7 @@
     when(lat == 0, clear_corner(0))
     when(lat == n_lat - 1, clear_corner(1))
 
+    get_windows.wait()
     rows_all, cols_all = 2 * n_lat, 2 * n_az
     lane = lax.broadcasted_iota(jnp.int32, (8, PAIR), 1)
     right_tile = lax.rem(lane // TS, 2)
@@ -259,49 +267,53 @@
             on = blocks[CORE, kind, rows(half)]
             beyond = blocks[off, kind, rows(half)]
             corner_out[index, kind] = jnp.where(from_on, on, beyond)
-        start(CORNER_UP, kind, (0,))
-        start(CORNER_DOWN, kind, (0,))
+        start(CORNER_UP, kind)
+        start(CORNER_DOWN, kind)
 
     get_q.wait()
     get_k.wait()
     add_keys(OWN, first=True)
+    relay(KEYS, 0)
     arrived(CORE, KEYS)
     add_keys(CORE)
-    relay(KEYS, 0)
-    start(TDIR, VALUES, (0,))
     relay(KEYS, 1)
-    start(TDIR, VALUES, (1,))
+    relay(KEYS, 2)
     arrived(UP, KEYS)
     arrived(DOWN, KEYS)
     add_keys(UP, DOWN)
+    relay(KEYS, 3)
     arrived(XREL, KEYS)
     send_corners(KEYS)
+    relay(VALUES, 0)
     add_keys(XREL)
-    relay(VALUES, 0)
-    arrived(TDIR, KEYS)
+    relay(VALUES, 1)
     arrived(TREL, KEYS)
-    add_keys(TDIR, TREL)
-    arrived(CORNER_UP, KEYS, (0,))
-    arrived(CORNER_DOWN, KEYS, (0,))
+    add_keys(TREL)
+    relay(VALUES, 2)
+    arrived(CORNER_UP, KEYS)
+    arrived(CORNER_DOWN, KEYS)
     add_keys(CORNER)
-    relay(VALUES, 1)
-    softmax()
+    relay(VALUES, 3)
     arrived(CORE, VALUES)
     arrived(XREL, VALUES)
     send_corners(VALUES)
+    arrived(TDIR, KEYS)
+    add_keys(TDIR)
+    softmax()
     arrived(UP, VALUES)
     arrived(DOWN, VALUES)
     get_v.wait()
     add_values(OWN, CORE, XREL, UP, DOWN, first=True)
-    arrived(CORNER_UP, VALUES, (0,))
-    arrived(CORNER_DOWN, VALUES, (0,))
+    arrived(CORNER_UP, VALUES)
+    arrived(CORNER_DOWN, VALUES)
     arrived(TREL, VALUES)
+    add_values(CORNER, TREL)
     arrived(TDIR, VALUES)
-    add_values(CORNER, TREL, TDIR, last=True)
+    add_values(TDIR, last=True)
     put = pltpu.make_async_copy(out, out_hbm.at[0], local_sem.at[0])
     put.start()
-    for name, kind, half in started:
-        when(routes[name][2], copy(name, kind, half).wait_send)
+    for name, kind, piece in started:
+        when(routes[name][2], copy(name, kind, piece).wait_send)
     put.wait()
 
 
@@ -316,9 +328,9 @@
             functools.partial(kernel, heads, n_az, n_lat, n_ta),
             out_shape=jax.ShapeDtypeStruct(queries.shape, queries.dtype),
             in_specs=[
-                pl.BlockSpec(memory_space=pltpu.SMEM),
-                pl.BlockSpec(memory_space=pl.ANY),
-                pl.BlockSpec(memory_space=pl.ANY),
+                pl.BlockSpec(memory_space=pltpu.HBM),
+                pl.BlockSpec(memory_space=pltpu.HBM),
+                pl.BlockSpec(memory_space=pltpu.HBM),
             ],
             out_specs=pl.BlockSpec(memory_space=pl.ANY),
             scratch_shapes=[
@@ -333,9 +345,10 @@
                 vmem((2, heads, PAIR, PAIR), jnp.float32),
                 vmem((2, heads, PAIR, HD), jnp.float32),
                 vmem((ROWS, COLS, width), jnp.bfloat16),
-                pltpu.SemaphoreType.DMA((len(TRANSFERS), 4)),
-                pltpu.SemaphoreType.DMA((len(TRANSFERS), 4)),
-                pltpu.SemaphoreType.DMA((3,)),
+                pltpu.SMEM(windows.shape, jnp.int32),
+                pltpu.SemaphoreType.DMA((len(TRANSFERS), 8)),
+                pltpu.SemaphoreType.DMA((len(TRANSFERS), 8)),
+                pltpu.SemaphoreType.DMA((4,)),
             ],
             compiler_params=pltpu.CompilerParams(
                 collective_id=0, has_side_effects=True, vmem_limit_bytes=56 * 2**20),

time: 72.7 us -> 66.9 us (0.920)
  the two profiles are of different devices: /device:TPU:152 before, /device:TPU:1 now
where the time goes in v2:
time: 66.9 us; the launch traced here: 66.7 us
  Pallas kernels  64.8 us (97%)
  local copies, waits for them, and re-layouts  1.88 us (3%)
    pallas_call x1, Pallas kernels, local(): pl.pallas_call(functools.partial(kernel, heads, n_az, n_lat, n_ta), out_s...  64.8 us
    unnamed x1, local copies, waits for them, and re-layouts  1.88 us

profile of v2, /device:TPU:1, one launch (start us, length us, event | category | flops | bytes accessed | tf_op | source)
XLA Modules:
  0.0 66.7 jit_solution(17152482913375919159)
XLA Ops:
  0.0 64.8 %tile_attention.1 = bf16[1,16,16,1024]{3,2,1,0:T(8,128)(2,1)} custom-call(s32[1,2,2,15]{3,2,1,0:T(2,128)} %windows_hbm.1, bf16[1,16,16,1024]{3,2,1,0:T(8,128)(2,1)} %q_hbm.1, bf16[2,1,16,16,1024]{4,3,2,1,0:T(8,128)(2,1)} %kv_hbm.1), custom_call_target="tpu_custom_call" | custom-call | tf_op jit(solution)/shard_map/tile_attention/pallas_call | solution.py:327
  64.8 1.9 %copy.5 = bf16[1,16,16,1024]{3,2,1,0:T(8,128)(2,1)} copy(bf16[1,16,16,1024]{3,2,1,0:T(8,128)(2,1)} %tile_attention.1) | data formatting | bytes 1048576

commit v3 on v2

--- a/solution.py
+++ b/solution.py
@@ -20,6 +20,7 @@
 PIECEWISE = (CROSS, XREL, TDIR, TREL)
 TRANSFERS = (CORE, CROSS, XREL, TDIR, TREL, UP, DOWN, CORNER_UP, CORNER_DOWN)
 KEYS, VALUES = 0, 1
+FRAME_STARTS = (1, 2, 3, 4, 6, 7, 8, 8)
 QUARTER = ROWS // 4
 
 CORNER = 8
@@ -46,7 +47,7 @@
 def kernel(
     heads, n_az, n_lat, n_ta, windows_hbm, q_hbm, kv_hbm, out_hbm,
     blocks, corner, corner_out, q, bias, scores, weights, peak, total, acc, out,
-    windows, send_sem, recv_sem, local_sem,
+    windows, send_sem, recv_sem, local_sem, frame_ready,
 ):
     az, lat, ta = lax.axis_index("az"), lax.axis_index("lat"), lax.axis_index("ta")
     place4 = lax.rem(az, 4)
@@ -74,13 +75,23 @@
     routes[CORNER_DOWN] = routes[DOWN]
 
     barrier = pltpu.get_barrier_semaphore()
+    sends_frame = routes[TREL][2]
     count = 0
-    for name in (CORE, CROSS, XREL, TDIR, TREL, UP, DOWN):
+    for name in (CORE, CROSS, XREL, UP, DOWN, TDIR, TREL):
         _, source, sends, receives = routes[name]
+        if name in (TDIR, TREL):
+            source = dict(source, az=source["az"] - lax.rem(source["az"], 2) + 1)
+        else:
+            count = count + (1 if sends is None else sends.astype(jnp.int32))
         when(receives, functools.partial(
             pl.semaphore_signal, barrier, inc=1, device_id=source, device_id_type=MESH))
-        count = count + (1 if sends is None else sends.astype(jnp.int32))
-    pl.semaphore_wait(barrier, count)
+    hears = sends_frame & (core == 1)
+    pl.semaphore_wait(barrier, count + jnp.where(hears, 4, 0))
+    when(hears, functools.partial(
+        pl.semaphore_signal, frame_ready, inc=1, device_id=routes[CORE][0], device_id_type=MESH))
+
+    def wait_frame():
+        when(sends_frame & (core == 0), functools.partial(pl.semaphore_wait, frame_ready, 1))
 
     def rows(half):
         return pl.ds(half * TS, TS)
@@ -118,11 +129,16 @@
         for piece in pieces(name) if some is None else some:
             when(routes[name][3], copy(name, kind, piece).wait_recv)
 
+    def send_frame(position):
+        for index, where in enumerate(FRAME_STARTS):
+            if where == position:
+                start(TDIR, index // 4, (index % 4,))
+
     def relay(kind, piece):
         arrived(CROSS, kind, (piece,))
         start(XREL, kind, (piece,))
         start(TREL, kind, (piece,))
-        start(TDIR, kind, (piece,))
+        send_frame(4 * kind + piece + 1)
 
     start(CROSS, KEYS)
     start(CROSS, VALUES)
@@ -192,7 +208,7 @@
             bias[r, :, c * 8:(c + 1) * 8, :] = jnp.where(listed, 0.0, NEG)
 
     off = jnp.where(outer, XREL, CROSS)
-    scale = 1.0 / math.sqrt(HD)
+    scale = math.log2(math.e) / math.sqrt(HD)
 
     def key_block(name, half, kind, columns):
         if name == CORNER:
@@ -220,7 +236,7 @@
                     best = score if best is None else jnp.maximum(best, score)
                 peak[r, h] = best
             return carry
-        lax.fori_loop(0, heads, head, 0)
+        lax.fori_loop(0, heads, head, 0, unroll=8)
 
     def softmax():
         def head(h, carry):
@@ -229,18 +245,18 @@
                 summed = None
                 for place in range(NPLACE):
                     part = slice(place * PAIR, (place + 1) * PAIR)
-                    weight = jnp.exp(scores[r, h, :, part] - most)
+                    weight = jnp.exp2(scores[r, h, :, part] - most)
                     weights[r, h, :, part] = weight.astype(jnp.bfloat16)
                     summed = weight if summed is None else summed + weight
                 total[r, h] = jnp.broadcast_to(
                     1.0 / jnp.sum(summed, axis=-1, keepdims=True), (PAIR, PAIR))
             return carry
-        lax.fori_loop(0, heads, head, 0)
-
-    def add_values(*names, first=False, last=False):
+        lax.fori_loop(0, heads, head, 0, unroll=8)
+
+    def add_values(*names, first=False, last=False, only=(0, 1)):
         def head(h, carry):
             columns = pl.ds(pl.multiple_of(h * HD, HD), HD)
-            for r in range(2):
+            for r in only:
                 result = None if first else acc[r, h]
                 for (name, half), place in PLACES[r].items():
                     if name not in names:
@@ -257,7 +273,7 @@
                 else:
                     acc[r, h] = result
             return carry
-        lax.fori_loop(0, heads, head, 0)
+        lax.fori_loop(0, heads, head, 0, unroll=8)
 
     left_half = lax.broadcasted_iota(jnp.int32, (TS, COLS, heads * HD), 1) < TS
 
@@ -272,6 +288,8 @@
 
     get_q.wait()
     get_k.wait()
+    wait_frame()
+    send_frame(0)
     add_keys(OWN, first=True)
     relay(KEYS, 0)
     arrived(CORE, KEYS)
@@ -282,39 +300,43 @@
     arrived(DOWN, KEYS)
     add_keys(UP, DOWN)
     relay(KEYS, 3)
+    relay(VALUES, 0)
+    relay(VALUES, 1)
     arrived(XREL, KEYS)
     send_corners(KEYS)
-    relay(VALUES, 0)
     add_keys(XREL)
-    relay(VALUES, 1)
+    relay(VALUES, 2)
+    relay(VALUES, 3)
+    arrived(TDIR, KEYS)
+    add_keys(TDIR)
     arrived(TREL, KEYS)
     add_keys(TREL)
-    relay(VALUES, 2)
     arrived(CORNER_UP, KEYS)
     arrived(CORNER_DOWN, KEYS)
     add_keys(CORNER)
-    relay(VALUES, 3)
+    softmax()
     arrived(CORE, VALUES)
     arrived(XREL, VALUES)
     send_corners(VALUES)
-    arrived(TDIR, KEYS)
-    add_keys(TDIR)
-    softmax()
     arrived(UP, VALUES)
     arrived(DOWN, VALUES)
     get_v.wait()
     add_values(OWN, CORE, XREL, UP, DOWN, first=True)
+    arrived(TREL, VALUES)
+    add_values(TREL)
     arrived(CORNER_UP, VALUES)
     arrived(CORNER_DOWN, VALUES)
-    arrived(TREL, VALUES)
-    add_values(CORNER, TREL)
-    arrived(TDIR, VALUES)
-    add_values(TDIR, last=True)
-    put = pltpu.make_async_copy(out, out_hbm.at[0], local_sem.at[0])
-    put.start()
+    add_values(CORNER)
+    puts = []
+    for r in range(2):
+        arrived(TDIR, VALUES, (2 * r, 2 * r + 1))
+        add_values(TDIR, last=True, only=(r,))
+        puts.append(pltpu.make_async_copy(out.at[rows(r)], out_hbm.at[0, rows(r)], local_sem.at[r]))
+        puts[r].start()
     for name, kind, piece in started:
         when(routes[name][2], copy(name, kind, piece).wait_send)
-    put.wait()
+    for put in puts:
+        put.wait()
 
 
 def solution(mesh):
@@ -349,6 +371,7 @@
                 pltpu.SemaphoreType.DMA((len(TRANSFERS), 8)),
                 pltpu.SemaphoreType.DMA((len(TRANSFERS), 8)),
                 pltpu.SemaphoreType.DMA((4,)),
+                pltpu.SemaphoreType.REGULAR,
             ],
             compiler_params=pltpu.CompilerParams(
                 collective_id=0, has_side_effects=True, vmem_limit_bytes=56 * 2**20),

time: 66.9 us -> 63.9 us (0.955)
  the two profiles are of different devices: /device:TPU:1 before, /device:TPU:28 now
where the time goes in v3:
time: 63.9 us; the launch traced here: 63.7 us
  Pallas kernels  61.9 us (97%)
  local copies, waits for them, and re-layouts  1.88 us (3%)
    pallas_call x1, Pallas kernels, local(): pl.pallas_call(functools.partial(kernel, heads, n_az, n_lat, n_ta), out_s...  61.9 us
    unnamed x1, local copies, waits for them, and re-layouts  1.88 us

profile of v3, /device:TPU:28, one launch (start us, length us, event | category | flops | bytes accessed | tf_op | source)
XLA Modules:
  0.0 63.7 jit_solution(5849689910364961954)
XLA Ops:
  0.0 61.9 %tile_attention.1 = bf16[1,16,16,1024]{3,2,1,0:T(8,128)(2,1)} custom-call(s32[1,2,2,15]{3,2,1,0:T(2,128)} %windows_hbm.1, bf16[1,16,16,1024]{3,2,1,0:T(8,128)(2,1)} %q_hbm.1, bf16[2,1,16,16,1024]{4,3,2,1,0:T(8,128)(2,1)} %kv_hbm.1), custom_call_target="tpu_custom_call" | custom-call | tf_op jit(solution)/shard_map/tile_attention/pallas_call | solution.py:349
  61.9 1.9 %copy.5 = bf16[1,16,16,1024]{3,2,1,0:T(8,128)(2,1)} copy(bf16[1,16,16,1024]{3,2,1,0:T(8,128)(2,1)} %tile_attention.1) | data formatting | bytes 1048576

commit v4 on v3

--- a/solution.py
+++ b/solution.py
@@ -45,8 +45,8 @@
 
 
 def kernel(
-    heads, n_az, n_lat, n_ta, windows_hbm, q_hbm, kv_hbm, out_hbm,
-    blocks, corner, corner_out, q, bias, scores, weights, peak, total, acc, out,
+    heads, n_az, n_lat, n_ta, windows_hbm, q_hbm, kv_hbm, out,
+    blocks, corner, corner_out, q, bias, scores, weights, peak, total, acc,
     windows, send_sem, recv_sem, local_sem, frame_ready,
 ):
     az, lat, ta = lax.axis_index("az"), lax.axis_index("lat"), lax.axis_index("ta")
@@ -269,7 +269,7 @@
                     result = part if result is None else result + part
                 if last:
                     result = (result * total[r, h]).astype(jnp.bfloat16)
-                    out[rows(r), :, columns] = result.reshape(TS, COLS, HD)
+                    out[0, rows(r), :, columns] = result.reshape(TS, COLS, HD)
                 else:
                     acc[r, h] = result
             return carry
@@ -327,16 +327,11 @@
     arrived(CORNER_UP, VALUES)
     arrived(CORNER_DOWN, VALUES)
     add_values(CORNER)
-    puts = []
     for r in range(2):
         arrived(TDIR, VALUES, (2 * r, 2 * r + 1))
         add_values(TDIR, last=True, only=(r,))
-        puts.append(pltpu.make_async_copy(out.at[rows(r)], out_hbm.at[0, rows(r)], local_sem.at[r]))
-        puts[r].start()
     for name, kind, piece in started:
         when(routes[name][2], copy(name, kind, piece).wait_send)
-    for put in puts:
-        put.wait()
 
 
 def solution(mesh):
@@ -348,13 +343,13 @@
         vmem = pltpu.VMEM
         return pl.pallas_call(
             functools.partial(kernel, heads, n_az, n_lat, n_ta),
-            out_shape=jax.ShapeDtypeStruct(queries.shape, queries.dtype),
+            out_shape=vmem(queries.shape, queries.dtype),
             in_specs=[
                 pl.BlockSpec(memory_space=pltpu.HBM),
                 pl.BlockSpec(memory_space=pltpu.HBM),
                 pl.BlockSpec(memory_space=pltpu.HBM),
             ],
-            out_specs=pl.BlockSpec(memory_space=pl.ANY),
+            out_specs=pl.BlockSpec(memory_space=pltpu.VMEM),
             scratch_shapes=[
                 vmem((8, 2, ROWS, COLS, width), jnp.bfloat16),
                 vmem((2, 2, TS, COLS, width), jnp.bfloat16),
@@ -366,7 +361,6 @@
                 vmem((2, heads, PAIR, PAIR), jnp.float32),
                 vmem((2, heads, PAIR, PAIR), jnp.float32),
                 vmem((2, heads, PAIR, HD), jnp.float32),
-                vmem((ROWS, COLS, width), jnp.bfloat16),
                 pltpu.SMEM(windows.shape, jnp.int32),
                 pltpu.SemaphoreType.DMA((len(TRANSFERS), 8)),
                 pltpu.SemaphoreType.DMA((len(TRANSFERS), 8)),
@@ -374,9 +368,9 @@
                 pltpu.SemaphoreType.REGULAR,
             ],
             compiler_params=pltpu.CompilerParams(
-                collective_id=0, has_side_effects=True, vmem_limit_bytes=56 * 2**20),
+                collective_id=0, has_side_effects=True, vmem_limit_bytes=40 * 2**20),
             name="tile_attention",
-        )(windows, queries, keys_values)
+        )(*[pltpu.with_memory_space_constraint(x, pltpu.HBM) for x in (windows, queries, keys_values)])
 
     return jax.shard_map(
         local,

time: 63.9 us -> 62.1 us (0.972)
  local copies, waits for them, and re-layouts: 1.88 us -> 0.8 us
  Pallas kernels: 61.9 us -> 61.2 us
    unnamed x1, local copies, waits for them, and re-layouts: 1.88 us -> 0.8 us
    pallas_call x1, Pallas kernels: 61.9 us -> 61.2 us  [local(): pl.pallas_call(functools.partial(kernel, heads, n_az, n_lat, n_ta), out_s...]
where the time goes in v4:
time: 62.1 us; the launch traced here: 62 us
  Pallas kernels  61.2 us (99%)
  local copies, waits for them, and re-layouts  0.8 us (1%)
    pallas_call x1, Pallas kernels, local(): pl.pallas_call(functools.partial(kernel, heads, n_az, n_lat, n_ta), out_s...  61.2 us

profile of v4, /device:TPU:28, one launch (start us, length us, event | category | flops | bytes accessed | tf_op | source)
XLA Modules:
  0.0 62.0 jit_solution(2642879235974665855)
XLA Ops:
  0.0 61.2 %tile_attention.1 = bf16[1,16,16,1024]{3,2,1,0:T(8,128)(2,1)S(1)} custom-call(s32[1,2,2,15]{3,2,1,0:T(2,128)} %windows_hbm.1, bf16[1,16,16,1024]{3,2,1,0:T(8,128)(2,1)} %q_hbm.1, bf16[2,1,16,16,1024]{4,3,2,1,0:T(8,128)(2,1)} %kv_hbm.1), custom_call_target="tpu_custom_call" | custom-call | tf_op jit(solution)/shard_map/tile_attention/pallas_call | solution.py:344
  61.2 0.8 %copy.5 = bf16[1,16,16,1024]{3,2,1,0:T(8,128)(2,1)} copy(bf16[1,16,16,1024]{3,2,1,0:T(8,128)(2,1)S(1)} %tile_attention.1) | data formatting | bytes 1048576

commit v5 on v4

--- a/solution.py
+++ b/solution.py
@@ -20,7 +20,11 @@
 PIECEWISE = (CROSS, XREL, TDIR, TREL)
 TRANSFERS = (CORE, CROSS, XREL, TDIR, TREL, UP, DOWN, CORNER_UP, CORNER_DOWN)
 KEYS, VALUES = 0, 1
-FRAME_STARTS = (1, 2, 3, 4, 6, 7, 8, 8)
+FRAME_STARTS = (
+    (0, 0, 1, 2, 5, 6, 7, 8),
+    (0, 0, 3, 4, 6, 7, 8, 8),
+    (1, 2, 3, 4, 6, 7, 8, 8),
+)
 QUARTER = ROWS // 4
 
 CORNER = 8
@@ -129,10 +133,22 @@
         for piece in pieces(name) if some is None else some:
             when(routes[name][3], copy(name, kind, piece).wait_recv)
 
+    lower = (step < 0) & (ta < n_ta - 2)
+    next_to_last = (step < 0) & (ta == n_ta - 2)
+    others = jnp.logical_not(lower | next_to_last)
+
     def send_frame(position):
-        for index, where in enumerate(FRAME_STARTS):
-            if where == position:
-                start(TDIR, index // 4, (index % 4,))
+        for index in range(8):
+            kind, piece = index // 4, index % 4
+            chosen = [
+                group for group, starts in zip((lower, next_to_last, others), FRAME_STARTS)
+                if starts[index] == position
+            ]
+            if chosen:
+                sends = routes[TDIR][2] & functools.reduce(jnp.logical_or, chosen)
+                pl.when(sends)(copy(TDIR, kind, piece).start)
+            if position == 8:
+                started.append((TDIR, kind, piece))
 
     def relay(kind, piece):
         arrived(CROSS, kind, (piece,))

time: 62.1 us -> 62.1 us (level)
  no operation moved by 1% of the time
where the time goes in v5:
time: 62.1 us; the launch traced here: 61.9 us
  Pallas kernels  61.1 us (98%)
  local copies, waits for them, and re-layouts  0.8 us (1%)
    pallas_call x1, Pallas kernels, local(): pl.pallas_call(functools.partial(kernel, heads, n_az, n_lat, n_ta), out_s...  61.1 us

profile of v5, /device:TPU:28, one launch (start us, length us, event | category | flops | bytes accessed | tf_op | source)
XLA Modules:
  0.0 61.9 jit_solution(3866073625969110964)
XLA Ops:
  0.0 61.1 %tile_attention.1 = bf16[1,16,16,1024]{3,2,1,0:T(8,128)(2,1)S(1)} custom-call(s32[1,2,2,15]{3,2,1,0:T(2,128)} %windows_hbm.1, bf16[1,16,16,1024]{3,2,1,0:T(8,128)(2,1)} %q_hbm.1, bf16[2,1,16,16,1024]{4,3,2,1,0:T(8,128)(2,1)} %kv_hbm.1), custom_call_target="tpu_custom_call" | custom-call | tf_op jit(solution)/shard_map/tile_attention/pallas_call | solution.py:360
  61.1 0.8 %copy.5 = bf16[1,16,16,1024]{3,2,1,0:T(8,128)(2,1)} copy(bf16[1,16,16,1024]{3,2,1,0:T(8,128)(2,1)S(1)} %tile_attention.1) | data formatting | bytes 1048576
